TPU v7x, 1024 devices: a whole 4x4x32 slice. The times are simulated.
1024 devices in a mesh: grp: 16 (over z_lo), dp: 64 (over y, z_hi, x, core).
Axes of the slice: x: 4, y: 4, z: 32 (z_hi: 2, z_lo: 16; z = z_hi * 16 + z_lo), core: 2. Of those that a mesh axis runs over, the one named last changes fastest.
Arguments:
- query_emb: bfloat16 [131072, 768], P(('grp', 'dp')), may hold values from -2 to 2
- passage_emb: bfloat16 [16384, 768], P(('grp', 'dp')), may hold values from -2 to 2
- positives: int32 [131072], P(('grp', 'dp')), may hold values from 0 to 1023
- hard_lists: int32 [16, 64, 4], P('grp', 'dp'), may hold values from 0 to 15, as said below
- hard_counts: int32 [16, 64], P('grp', 'dp'), may hold values from 1 to 4
Outputs:
- question_derivative: bfloat16 [131072, 768], P(('grp', 'dp'))
- passage_grad: bfloat16 [16384, 768], P(('grp', 'dp'))
- losses: float32 [131072], P(('grp', 'dp'))
Inputs may be any that keep to these rules, and one draw needn't show every extreme that they name: `hard_lists`: the entries of one device's list are distinct and never its own group.
All inputs are finite; a program needn't handle non-finite values.
Results may differ from a plain program's by a relative error of at most 0.0055.
Values may be sent and summed in bfloat16 or wider, within the bound.
A program may use at most 32 MiB of HBM per device.

v0:
```python
import jax
import jax.numpy as jnp
from jax import lax
from jax.sharding import PartitionSpec as P

inverse_softmax_scale = 20.0
dead_score = -1e30


def per_device(query_emb, passage_emb, positives, hard_lists, hard_counts):
    group_count = lax.axis_size("grp")
    block_rows = passage_emb.shape[0]
    inside = lax.all_gather(passage_emb, "dp", axis=0, tiled=True)
    remote = lax.all_gather(passage_emb, "grp", axis=0, tiled=True)
    chosen = hard_lists.reshape(-1)
    hard_number = hard_counts.reshape(())
    slot_ids = jnp.arange(chosen.shape[0], dtype=jnp.int32)
    live_slots = slot_ids < hard_number
    slot_table = (
        chosen[:, None] == jnp.arange(group_count, dtype=jnp.int32)[None, :]
    ) & live_slots[:, None]
    keep_cols = jnp.repeat(jnp.any(slot_table, axis=0), block_rows)
    contract_last = (((1,), (1,)), ((), ()))
    contract_first = (((0,), (0,)), ((), ()))
    batch_passage_logit = (
        lax.dot_general(query_emb, inside, contract_last, preferred_element_type=jnp.float32)
        * inverse_softmax_scale
    )
    mined_passage_logit = (
        lax.dot_general(query_emb, remote, contract_last, preferred_element_type=jnp.float32)
        * inverse_softmax_scale
    )
    mined_passage_logit = jnp.where(keep_cols[None, :], mined_passage_logit, dead_score)
    row_max = jnp.maximum(
        jnp.max(batch_passage_logit, axis=1), jnp.max(mined_passage_logit, axis=1)
    )
    total = jnp.sum(jnp.exp(batch_passage_logit - row_max[:, None]), axis=1) + jnp.sum(
        jnp.exp(mined_passage_logit - row_max[:, None]), axis=1
    )
    log_total = row_max + jnp.log(total)
    column_ids = jnp.arange(inside.shape[0], dtype=jnp.int32)
    hit_mask = column_ids[None, :] == positives[:, None]
    pos_score = jnp.sum(jnp.where(hit_mask, batch_passage_logit, 0.0), axis=1)
    losses = log_total - pos_score
    batch_passage_derivative = (
        jnp.exp(batch_passage_logit - log_total[:, None]) - hit_mask.astype(jnp.float32)
    ).astype(jnp.bfloat16)
    mined_passage_derivative = jnp.exp(mined_passage_logit - log_total[:, None]).astype(
        jnp.bfloat16
    )
    question_derivative = (
        jnp.dot(batch_passage_derivative, inside, preferred_element_type=jnp.float32)
        + jnp.dot(mined_passage_derivative, remote, preferred_element_type=jnp.float32)
    ) * inverse_softmax_scale
    mined_passage_addend = (
        lax.dot_general(
            mined_passage_derivative, query_emb, contract_first, preferred_element_type=jnp.float32
        )
        * inverse_softmax_scale
    )
    hard_share = lax.psum_scatter(
        mined_passage_addend.astype(jnp.bfloat16), "grp", scatter_dimension=0, tiled=True
    ).astype(jnp.float32)
    batch_passage_addend = (
        lax.dot_general(
            batch_passage_derivative, query_emb, contract_first, preferred_element_type=jnp.float32
        )
        * inverse_softmax_scale
    )
    own_share = lax.psum_scatter(batch_passage_addend, "dp", scatter_dimension=0, tiled=True)
    passage_grad = (own_share + hard_share).astype(jnp.bfloat16)
    return (question_derivative.astype(jnp.bfloat16), passage_grad, losses)


def solution(mesh):
    in_specs = (
        P(("grp", "dp"), None),
        P(("grp", "dp"), None),
        P(("grp", "dp")),
        P("grp", "dp", None),
        P("grp", "dp"),
    )
    out_specs = (P(("grp", "dp"), None), P(("grp", "dp"), None), P(("grp", "dp")))
    return jax.shard_map(
        per_device, mesh=mesh, in_specs=in_specs, out_specs=out_specs, check_vma=False
    )
```

profile of v0, /device:TPU:1, one launch (start us, length us, event | category | flops | bytes accessed | tf_op | source)
XLA Modules:
  0.0 653.1 jit_solution(7458650391614270293)
XLA Ops:
  7.2 0.0 all-gather.2.cloned.1.call-start
  7.2 0.7 all-gather.2.cloned.1.call-update
  7.9 0.0 reduce-scatter.5.cloned.1.call-start
  8.6 0.7 fusion.5
  9.4 0.1 broadcast_in_dim.29
  9.4 0.1 broadcast_in_dim.30
  9.5 108.0 %all_gather.7 = bf16[256,768]{1,0:T(8,128)(2,1)S(1)} all-gather(bf16[16,768]{1,0:T(8,128)(2,1)} %param.6), channel_id=1, replica_groups=mesh['grp'=16,'dp'=64] {'grp'}, dimensions={0}, use_global_device_ids=true | all-gather | bytes 417792 | tf_op jit(solution)/shard_map/all_gather | solution.py:14
  117.5 0.4 fusion.9
  117.9 67.9 %all-gather.2.cloned.1.call-done = bf16[1024,768]{1,0:T(8,128)(2,1)} async-done(((bf16[16,768]{1,0:T(8,128)(2,1)}), bf16[1024,768]{1,0:T(8,128)(2,1)}) %all-gather.2.cloned.1.call-update) | async-done | bytes 1572880 | tf_op jit(solution)/shard_map/all_gather | solution.py:13
  185.8 2.1 fusion.8
  187.9 0.2 exponential_reduce_fusion.1
  188.1 0.3 select_reduce_fusion
  188.4 0.5 fusion.7
  188.9 1.1 fusion
  190.1 0.0 reduce-scatter.5.cloned.1.call-update
  190.1 0.0 reduce-scatter.3.cloned.1.call-start
  190.1 2.4 convolution_multiply_fusion
  192.5 0.0 reduce-scatter.3.cloned.1.call-update
  192.5 1.4 copy-done.1
  193.9 0.5 fusion.6
  194.4 0.9 fusion.2
  195.3 160.0 %reduce-scatter.5.cloned.1.call-done = bf16[16,768]{1,0:T(8,128)(2,1)} async-done(((bf16[256,768]{1,0:T(8,128)(2,1)}), bf16[16,768]{1,0:T(8,128)(2,1)}) %reduce-scatter.5.cloned.1.call-update) | async-done | bytes 24592 | tf_op jit(solution)/shard_map/reduce_scatter | solution.py:61
  355.3 289.9 %reduce-scatter.3.cloned.1.call-done = f32[16,768]{1,0:T(8,128)} async-done(((f32[1024,768]{1,0:T(8,128)}), f32[16,768]{1,0:T(8,128)}) %reduce-scatter.3.cloned.1.call-update) | async-done | bytes 49168 | tf_op jit(solution)/shard_map/reduce_scatter | solution.py:70
  645.1 1.4 add_convert_fusion
  (7 shorter events, 0.0 us)
Async XLA Ops:
  7.2 110.4 %copy-start = (bf16[128,768]{1,0:T(8,128)(2,1)S(1)}, bf16[128,768]{1,0:T(8,128)(2,1)}, u32[]{:S(2)}) copy-start(bf16[128,768]{1,0:T(8,128)(2,1)} %param.5) | copy-start | bytes 589828
  7.2 178.6 %all-gather.2.cloned.1.call-start = ((), (), s32[]{:S(2)}) async-start(), calls=%async_computation.2 | async-start | bytes 1597440 | tf_op jit(solution)/shard_map/all_gather | solution.py:13
  7.9 347.4 %reduce-scatter.5.cloned.1.call-start = ((), (), s32[]{:S(2)}) async-start(), calls=%async_computation.4 | async-start | bytes 417792 | tf_op jit(solution)/shard_map/reduce_scatter | solution.py:61
  117.5 70.6 %copy-start.2 = (s32[128]{0:T(128)S(1)}, s32[128]{0:T(128)}, u32[]{:S(2)}) copy-start(s32[128]{0:T(128)} %param.7) | copy-start | bytes 1540
  190.1 455.1 %reduce-scatter.3.cloned.1.call-start = ((), (), s32[]{:S(2)}) async-start(), calls=%async_computation.3 | async-start | bytes 3194880 | tf_op jit(solution)/shard_map/reduce_scatter | solution.py:70
  192.5 1.4 copy-start.1
Sparse Core Ops, SparseCore 0:
  13.8 171.9 all-gather.1
  190.2 165.0 reduce-scatter.4
  362.9 282.2 reduce-scatter.2
where the time goes:
time: 653 us
  waiting for transfers between devices  518 us (79%)
  blocking collectives  108 us (17%)
  between operations  14.4 us (2%)
  matrix products  7.4 us (1%)
    reduce_scatter x1, waiting for transfers between devices, per_device(): lax.psum_scatter(batch_passage_addend, 'dp', scatter_dimension=0, tiled=T...  290 us
    reduce_scatter x1, waiting for transfers between devices, per_device(): lax.psum_scatter(mined_passage_addend.astype(jnp.bfloat16), 'grp', scatte...  160 us
    all_gather x1, blocking collectives, per_device(): remote = lax.all_gather(passage_emb, 'grp', axis=0, tiled=True)  108 us
    all_gather x1, waiting for transfers between devices, per_device(): inside = lax.all_gather(passage_emb, 'dp', axis=0, tiled=True)  67.9 us
  transfers between devices with their start and end apart: 3, of which 3 were waited for; matrix products, arithmetic and copies ran while one was open for 1% of the time, Pallas kernels for 0%

commit v1 on v0

v1 whole, which is shorter than its diff:
```python
import jax
import jax.numpy as jnp
from jax import lax
from jax.experimental import pallas as pl
from jax.experimental.pallas import tpu as pltpu
from jax.sharding import PartitionSpec as P

MESH = pl.DeviceIdType.MESH
SCALE = 20.0
DEAD = -1e30
GROUPS = 16
ROWS = 16
QUERIES = 128
WIDTH = 768
HUBS = (-2, -1, 1, 2)
NEAR = (-1, 1, -2, 2, -3, 3, -4, 4, -5, 5)
SHIFTS = tuple((dy, dx) for dy in range(4) for dx in range(4) if (dy, dx) != (0, 0))


def inside(h):
    return (h >= 0) & (h < GROUPS)


def is_leaf(k, e, hub):
    ok = inside(hub - 5 * k) & inside(hub + e)
    if abs(e) <= 2:
        return ok
    if (e > 0 and k < 0) or (e < 0 and k > 0):
        return None
    if abs(k) == 2:
        return ok
    return ok & ((hub >= 11) if e > 0 else (hub <= 4))


def is_relay(k, hub):
    if k == 2:
        return hub >= 10
    if k == -2:
        return hub <= 5
    if k == 1:
        return (hub == 13) | (hub == 14)
    return (hub == 1) | (hub == 2)


def rows_of(index):
    return pl.ds(pl.multiple_of(index * ROWS, ROWS), ROWS)


def score(a, b):
    return SCALE * lax.dot_general(
        a, b, (((1,), (1,)), ((), ())), preferred_element_type=jnp.float32
    )


def over_rows(a, b):
    return lax.dot_general(a, b, (((0,), (0,)), ((), ())), preferred_element_type=jnp.float32)


def dot(a, b):
    return jnp.dot(a, b, preferred_element_type=jnp.float32)


def kernel(
    q_in, p_in, pos_in, lists, counts,
    dq_out, dp_out, loss_out,
    q_buf, pos_own, pos_sib, p_buf, o_buf, s_buf, so_buf, g_buf, go_buf,
    st_mine, st_sib, dq_mine, dq_send, dq_sib,
    d_buf, r_buf, do_buf, leaf_buf, hub_buf, sum_buf, relay_buf, far_buf, acc,
    loc_sem, line_recv, hub_send, leaf_send, relay_send, far_recv, plane_send, plane_recv,
    sib_send, sib_recv, d_send, d_recv, leaf_send2, leaf_recv2, hub_send2, hub_recv2,
    sum_send, relay_recv2, relay_send2, far_recv2,
):
    g = lax.axis_index("grp")
    d = lax.axis_index("dp")
    y, zh, x, c = d // 16, (d // 8) % 2, (d // 2) % 4, d % 2

    def at(yy, zz, xx, cc):
        return ((yy * 2 + zz) * 4 + xx) * 2 + cc

    sib = (g, at(y, zh, x, 1 - c))
    plane = [(g, at((y + dy) % 4, zh, (x + dx) % 4, c)) for dy, dx in SHIFTS]
    far_dp = at(y, 1 - zh, x, c)
    my_slot = y * 4 + x
    my_k = jnp.where(g <= 5, 2, jnp.where(g <= 7, -1, jnp.where(g <= 9, 1, -2)))
    my_relay = g + 5 * my_k

    def copy(src, dst, send, recv, dev):
        return pltpu.make_async_remote_copy(
            src_ref=src, dst_ref=dst, send_sem=send, recv_sem=recv,
            device_id=dev, device_id_type=MESH,
        )

    def received(dst, sem):
        copy(dst, dst, sem, sem, sib).wait_recv()

    def sent(src, sem):
        copy(src, src, sem, sem, sib).wait_send()

    barrier = pltpu.get_barrier_semaphore()

    def tell(dev):
        pl.semaphore_signal(barrier, inc=1, device_id=dev, device_id_type=MESH)

    expected = jnp.int32(1 + len(SHIFTS))
    for o in (-10, 10, -5, 5, -4, 4, -3, 3, -2, 2, -1, 1):
        ok = inside(g + o)
        pl.when(ok)(lambda o=o: tell((g + o, d)))
        expected = expected + ok.astype(jnp.int32)
    tell((my_relay, far_dp))
    for k in HUBS:
        expected = expected + is_relay(k, g).astype(jnp.int32)
    for dev in plane:
        tell(dev)
    tell(sib)

    own = p_buf.at[rows_of(my_slot)]
    local = [
        pltpu.make_async_copy(p_in, own, loc_sem.at[0]),
        pltpu.make_async_copy(p_in, o_buf.at[rows_of(g)], loc_sem.at[1]),
        pltpu.make_async_copy(q_in, q_buf.at[pl.ds(0, QUERIES)], loc_sem.at[2]),
        pltpu.make_async_copy(pos_in, pos_own, loc_sem.at[3]),
    ]
    for cp in local:
        cp.start()
    for cp in local:
        cp.wait()
    pl.semaphore_wait(barrier, expected)

    def hub_copy(i, k):
        return copy(own, o_buf.at[rows_of(g)], hub_send.at[i], line_recv.at[g], (g + 5 * k, d))

    def leaf_copy(kk, k, j, e):
        block = o_buf.at[rows_of(g - 5 * k)]
        return copy(block, block, leaf_send.at[kk, j], line_recv.at[g - 5 * k], (g + e, d))

    def leaf_starts(kk, k):
        for j, e in enumerate(NEAR):
            ok = is_leaf(k, e, g)
            if ok is not None:
                pl.when(ok)(lambda kk=kk, k=k, j=j, e=e: leaf_copy(kk, k, j, e).start())

    def far_copy(i, k):
        return copy(
            o_buf.at[rows_of(g - 5 * k)], p_buf.at[rows_of(16 + my_slot)],
            relay_send.at[i], far_recv.at[0], (g - 5 * k, far_dp),
        )

    def plane_copy(part, i):
        block = p_buf.at[rows_of(part * 16 + my_slot)]
        return copy(block, block, plane_send.at[part, i], plane_recv.at[part, i], plane[i])

    for i, k in ((0, -2), (3, 2), (1, -1), (2, 1)):
        pl.when(inside(g + 5 * k))(lambda i=i, k=k: hub_copy(i, k).start())
    for i in range(15):
        plane_copy(0, i).start()
    leaf_starts(2, 0)
    q_copy = copy(
        q_buf.at[pl.ds(0, QUERIES)], q_buf.at[pl.ds(QUERIES, QUERIES)],
        sib_send.at[0], sib_recv.at[0], sib,
    )
    pos_copy = copy(pos_own, pos_sib, sib_send.at[1], sib_recv.at[1], sib)
    q_copy.start()
    pos_copy.start()

    for i, k, kk in ((1, -1, 1), (2, 1, 3), (0, -2, 0), (3, 2, 4)):

        @pl.when(inside(g - 5 * k))
        def _(i=i, k=k, kk=kk):
            received(o_buf.at[rows_of(g - 5 * k)], line_recv.at[g - 5 * k])
            pl.when(is_relay(k, g))(lambda: far_copy(i, k).start())
            leaf_starts(kk, k)

    q_copy.wait_recv()
    pos_copy.wait_recv()
    for i in range(15):
        plane_copy(0, i).wait_recv()
    s_buf[0:256] = score(p_buf[0:256], q_buf[...])

    received(p_buf.at[rows_of(16 + my_slot)], far_recv.at[0])
    for i in range(15):
        plane_copy(1, i).start()

    for o in range(1, GROUPS):
        h = (g + o) % GROUPS
        direct = False
        for k in HUBS:
            direct = direct | (h == g - 5 * k)
        pl.when(jnp.logical_not(direct))(
            lambda h=h: received(o_buf.at[rows_of(h)], line_recv.at[h])
        )
    row_group = lax.broadcasted_iota(jnp.int32, (GROUPS * ROWS, QUERIES), 0) >> 4
    live = jnp.zeros((GROUPS * ROWS, QUERIES), jnp.bool_)
    for i in range(4):
        entry = jnp.where(i < counts[0, 0], lists[0, i], -1)
        live = live | (row_group == entry)
    outer = jnp.where(live, score(o_buf[...], q_buf[0:QUERIES]), DEAD)
    so_buf[...] = outer
    outer_max = jnp.max(outer, axis=0, keepdims=True)
    outer_sum = jnp.sum(jnp.exp(outer - outer_max), axis=0, keepdims=True)

    for i in range(15):
        plane_copy(1, i).wait_recv()
    s_buf[256:512] = score(p_buf[256:512], q_buf[...])

    pos = jnp.concatenate([pos_own[...], pos_sib[...]], axis=1)

    def hits(part):
        i = lax.broadcasted_iota(jnp.int32, (256, 2 * QUERIES), 0)
        zz = zh + part - 2 * zh * part
        column = ((i >> 6) << 8) + zz * 128 + (((i >> 4) & 3) << 5) + c * 16 + (i & 15)
        return column == pos

    s0, s1 = s_buf[0:256], s_buf[256:512]
    top = jnp.maximum(jnp.max(s0, axis=0, keepdims=True), jnp.max(s1, axis=0, keepdims=True))
    total = jnp.sum(jnp.exp(s0 - top), axis=0, keepdims=True) + jnp.sum(
        jnp.exp(s1 - top), axis=0, keepdims=True
    )
    picked = jnp.sum(jnp.where(hits(0), s0, 0.0), axis=0, keepdims=True) + jnp.sum(
        jnp.where(hits(1), s1, 0.0), axis=0, keepdims=True
    )
    own_top = jnp.maximum(top[:, :QUERIES], outer_max)
    own_total = total[:, :QUERIES] * jnp.exp(top[:, :QUERIES] - own_top) + outer_sum * jnp.exp(
        outer_max - own_top
    )
    top = jnp.concatenate([own_top, top[:, QUERIES:]], axis=1)
    total = jnp.concatenate([own_total, total[:, QUERIES:]], axis=1)
    st_mine[0:1] = top
    st_mine[1:2] = total
    st_mine[2:3] = picked
    st_mine[3:8] = jnp.zeros((5, 2 * QUERIES), jnp.float32)
    st_copy = copy(st_mine, st_sib, sib_send.at[2], sib_recv.at[2], sib)
    st_copy.start()

    for i, k in enumerate(HUBS):
        pl.when(inside(g + 5 * k))(lambda i=i, k=k: hub_copy(i, k).wait_send())

        @pl.when(inside(g - 5 * k))
        def _(i=i, k=k):
            pl.when(is_relay(k, g))(lambda: far_copy(i, k).wait_send())

    for kk in range(5):
        for j, e in enumerate(NEAR):
            ok = is_leaf(kk - 2, e, g)
            if ok is not None:
                pl.when(ok)(lambda kk=kk, j=j, e=e: leaf_copy(kk, kk - 2, j, e).wait_send())
    for i in range(15):
        plane_copy(0, i).wait_send()
        plane_copy(1, i).wait_send()
    q_copy.wait_send()
    pos_copy.wait_send()

    st_copy.wait()
    swapped = jnp.concatenate([st_sib[:, QUERIES:], st_sib[:, :QUERIES]], axis=1)
    both_top = jnp.maximum(top, swapped[0:1])
    both = total * jnp.exp(top - both_top) + swapped[1:2] * jnp.exp(swapped[0:1] - both_top)
    log_total = both_top + jnp.log(both)
    loss_out[...] = (log_total - (picked + swapped[2:3]))[:, :QUERIES]

    def part_grad(part):
        a = jnp.exp(s_buf[part * 256 : part * 256 + 256] - log_total)
        a = (a - hits(part).astype(jnp.float32)).astype(jnp.bfloat16)
        g_buf[part * 256 : part * 256 + 256] = a
        d_buf[part * 256 : part * 256 + 256] = (SCALE * dot(a, q_buf[...])).astype(jnp.bfloat16)

    def d_copy(part, i):
        dy, dx = SHIFTS[i]
        slot = part * 16 + ((y + dy) % 4) * 4 + (x + dx) % 4
        return copy(
            d_buf.at[rows_of(slot)], r_buf.at[part, i], d_send.at[part, i], d_recv.at[part, i],
            plane[i],
        )

    def leaf_back(kk, k, j, e):
        return copy(
            do_buf.at[rows_of(g - e - 5 * k)], leaf_buf.at[kk, j], leaf_send2.at[kk, j],
            leaf_recv2.at[kk, j], (g - e, d),
        )

    part_grad(1)
    for i in range(15):
        d_copy(1, i).start()
    a = jnp.where(live, jnp.exp(so_buf[...] - log_total[:, :QUERIES]), 0.0).astype(jnp.bfloat16)
    go_buf[...] = a
    do_buf[...] = (SCALE * dot(a, q_buf[0:QUERIES])).astype(jnp.bfloat16)
    for kk in (0, 4, 1, 3, 2):
        for j, e in enumerate(NEAR):
            ok = is_leaf(kk - 2, e, g - e)
            if ok is not None:
                ok = ok & inside(g - e)
                pl.when(ok)(lambda kk=kk, j=j, e=e: leaf_back(kk, kk - 2, j, e).start())
    part_grad(0)
    for i in range(15):
        d_copy(0, i).start()

    dq_send[...] = over_rows(g_buf[:, QUERIES:], p_buf[...])
    dq_copy = copy(dq_send, dq_sib, sib_send.at[3], sib_recv.at[3], sib)
    dq_copy.start()

    def add_leaves(kk, k):
        for j, e in enumerate(NEAR):
            ok = is_leaf(k, e, g)
            if ok is not None:

                @pl.when(ok)
                def _(kk=kk, j=j):
                    received(leaf_buf.at[kk, j], leaf_recv2.at[kk, j])
                    acc[...] += leaf_buf[kk, j].astype(jnp.float32)

    def hub_back(i, k):
        return copy(
            sum_buf.at[i], hub_buf.at[i], hub_send2.at[i], hub_recv2.at[i], (g - 5 * k, d)
        )

    def add_hub(i, k, kk):
        @pl.when(inside(g - 5 * k))
        def _():
            acc[...] = do_buf[rows_of(g - 5 * k)].astype(jnp.float32)
            add_leaves(kk, k)
            sum_buf[i] = acc[...].astype(jnp.bfloat16)
            hub_back(i, k).start()

    add_hub(0, -2, 0)
    add_hub(3, 2, 4)

    total_far = d_buf[rows_of(16 + my_slot)].astype(jnp.float32)
    for i in range(15):
        d_copy(1, i).wait_recv()
        total_far = total_far + r_buf[1, i].astype(jnp.float32)
    sum_buf[4] = total_far.astype(jnp.bfloat16)
    for i, k in enumerate(HUBS):

        @pl.when(my_k == k)
        def _(i=i, k=k):
            copy(
                sum_buf.at[4], relay_buf.at[i], sum_send.at[0], relay_recv2.at[i], (g + 5 * k, d)
            ).start()

    add_hub(1, -1, 1)
    add_hub(2, 1, 3)

    def relay_back(i, k):
        return copy(
            relay_buf.at[i], far_buf, relay_send2.at[i], far_recv2.at[0], (g - 5 * k, far_dp)
        )

    for i, k in enumerate(HUBS):

        @pl.when(is_relay(k, g))
        def _(i=i, k=k):
            received(relay_buf.at[i], relay_recv2.at[i])
            relay_back(i, k).start()

    dq_mine[...] = over_rows(g_buf[:, :QUERIES], p_buf[...]) + over_rows(go_buf[...], o_buf[...])
    dq_copy.wait_recv()
    dq_out[...] = (SCALE * (dq_mine[...] + dq_sib[...])).astype(jnp.bfloat16)

    acc[...] = d_buf[rows_of(my_slot)].astype(jnp.float32) + do_buf[rows_of(g)].astype(jnp.float32)
    for i in range(15):
        d_copy(0, i).wait_recv()
        acc[...] += r_buf[0, i].astype(jnp.float32)
    add_leaves(2, 0)
    for i, k in enumerate(HUBS):

        @pl.when(inside(g + 5 * k))
        def _(i=i, k=k):
            received(hub_buf.at[i], hub_recv2.at[i])
            acc[...] += hub_buf[i].astype(jnp.float32)

    received(far_buf, far_recv2.at[0])
    dp_out[...] = (acc[...] + far_buf[...].astype(jnp.float32)).astype(jnp.bfloat16)

    for i in range(15):
        d_copy(0, i).wait_send()
        d_copy(1, i).wait_send()
    for kk in range(5):
        for j, e in enumerate(NEAR):
            ok = is_leaf(kk - 2, e, g - e)
            if ok is not None:
                ok = ok & inside(g - e)
                pl.when(ok)(lambda kk=kk, j=j, e=e: leaf_back(kk, kk - 2, j, e).wait_send())
    for i, k in enumerate(HUBS):
        pl.when(inside(g - 5 * k))(lambda i=i, k=k: hub_back(i, k).wait_send())
        pl.when(is_relay(k, g))(lambda i=i, k=k: relay_back(i, k).wait_send())
    sent(sum_buf.at[4], sum_send.at[0])
    dq_copy.wait_send()


def per_device(query_emb, passage_emb, positives, hard_lists, hard_counts):
    bf16, f32, i32 = jnp.bfloat16, jnp.float32, jnp.int32
    dma = pltpu.SemaphoreType.DMA
    block = (ROWS, WIDTH)
    anywhere = pl.BlockSpec(memory_space=pl.ANY)
    smem = pl.BlockSpec(memory_space=pltpu.SMEM)
    vmem = pl.BlockSpec(memory_space=pltpu.VMEM)
    dq, dp, loss = pl.pallas_call(
        kernel,
        out_shape=(
            jax.ShapeDtypeStruct((QUERIES, WIDTH), bf16),
            jax.ShapeDtypeStruct(block, bf16),
            jax.ShapeDtypeStruct((1, QUERIES), f32),
        ),
        in_specs=[anywhere, anywhere, anywhere, smem, smem],
        out_specs=(vmem, vmem, vmem),
        scratch_shapes=[
            pltpu.VMEM((2 * QUERIES, WIDTH), bf16),
            pltpu.VMEM((1, QUERIES), i32),
            pltpu.VMEM((1, QUERIES), i32),
            pltpu.VMEM((512, WIDTH), bf16),
            pltpu.VMEM((256, WIDTH), bf16),
            pltpu.VMEM((512, 2 * QUERIES), f32),
            pltpu.VMEM((256, QUERIES), f32),
            pltpu.VMEM((512, 2 * QUERIES), bf16),
            pltpu.VMEM((256, QUERIES), bf16),
            pltpu.VMEM((8, 2 * QUERIES), f32),
            pltpu.VMEM((8, 2 * QUERIES), f32),
            pltpu.VMEM((QUERIES, WIDTH), f32),
            pltpu.VMEM((QUERIES, WIDTH), f32),
            pltpu.VMEM((QUERIES, WIDTH), f32),
            pltpu.VMEM((512, WIDTH), bf16),
            pltpu.VMEM((2, 15) + block, bf16),
            pltpu.VMEM((256, WIDTH), bf16),
            pltpu.VMEM((5, 10) + block, bf16),
            pltpu.VMEM((4,) + block, bf16),
            pltpu.VMEM((5,) + block, bf16),
            pltpu.VMEM((4,) + block, bf16),
            pltpu.VMEM(block, bf16),
            pltpu.VMEM(block, f32),
            dma((4,)),
            dma((16,)),
            dma((4,)),
            dma((5, 10)),
            dma((4,)),
            dma((1,)),
            dma((2, 15)),
            dma((2, 15)),
            dma((4,)),
            dma((4,)),
            dma((2, 15)),
            dma((2, 15)),
            dma((5, 10)),
            dma((5, 10)),
            dma((4,)),
            dma((4,)),
            dma((1,)),
            dma((4,)),
            dma((4,)),
            dma((1,)),
        ],
        name="dual_encoder",
        compiler_params=pltpu.CompilerParams(
            collective_id=0, has_side_effects=True, vmem_limit_bytes=40 * 1024 * 1024
        ),
    )(
        query_emb, passage_emb, positives.reshape(1, QUERIES), hard_lists.reshape(1, 4),
        hard_counts,
    )
    return dq, dp, loss.reshape(QUERIES)


def solution(mesh):
    in_specs = (
        P(("grp", "dp"), None),
        P(("grp", "dp"), None),
        P(("grp", "dp")),
        P("grp", "dp", None),
        P("grp", "dp"),
    )
    out_specs = (P(("grp", "dp"), None), P(("grp", "dp"), None), P(("grp", "dp")))
    return jax.shard_map(
        per_device, mesh=mesh, in_specs=in_specs, out_specs=out_specs, check_vma=False
    )
```

time: 653 us -> 88.8 us (0.14)
  the two profiles are of different devices: /device:TPU:1 before, /device:TPU:64 now
where the time goes in v1:
time: 88.8 us; the launch traced here: 88.6 us
  Pallas kernels  83.2 us (94%)
  local copies, waits for them, and re-layouts  4.12 us (5%)
  between operations  1.31 us (1%)
    pallas_call x1, Pallas kernels, per_device(): pl.pallas_call(kernel, out_shape=(jax.ShapeDtypeStruct((QUERIES, WIDTH),...  83.2 us
    unnamed x11, local copies, waits for them, and re-layouts  4.12 us

profile of v1, /device:TPU:64, one launch (start us, length us, event | category | flops | bytes accessed | tf_op | source)
XLA Modules:
  0.0 88.6 jit_solution(14748271316728633302)
XLA Ops:
  1.3 0.0 copy-start.2
  1.3 0.0 copy-start.3
  1.3 0.6 copy-done.2
  1.9 0.0 copy-done.3
  1.9 0.0 copy-start
  2.0 0.9 %copy-done = bf16[128,768]{1,0:T(8,128)(2,1)S(1)} copy-done((bf16[128,768]{1,0:T(8,128)(2,1)S(1)}, bf16[128,768]{1,0:T(8,128)(2,1)}, u32[]{:S(2)}) %copy-start) | copy-done | bytes 196632
  2.9 0.0 copy-start.1
  2.9 0.7 copy-done.1
  3.6 83.2 %dual_encoder.1 = (bf16[128,768]{1,0:T(8,128)(2,1)S(1)}, bf16[16,768]{1,0:T(8,128)(2,1)S(1)}, f32[1,128]{1,0:T(1,128)S(1)}) custom-call(bf16[128,768]{1,0:T(8,128)(2,1)S(1)} %copy-done, bf16[16,768]{1,0:T(8,128)(2,1)S(1)} %copy-done.1, s32[1,128]{1,0:T(1,128)S(1)} %bitcast.3, s32[1,4]{1,0:T(1,128)S(1)} %bitcast.4, s32[1,1]{1,0:T(1,128)S(6)} %copy.11.counts), custom_call_target="tpu_custom_call" | custom-call | tf_op jit(solution)/shard_map/dual_encoder/pallas_call | solution.py:395
  86.8 0.7 copy.12
  87.5 0.6 copy.13
  88.1 0.5 copy.14
Async XLA Ops:
  1.3 0.7 copy-start.2
  1.3 0.7 copy-start.3
  1.9 0.9 %copy-start = (bf16[128,768]{1,0:T(8,128)(2,1)S(1)}, bf16[128,768]{1,0:T(8,128)(2,1)}, u32[]{:S(2)}) copy-start(bf16[128,768]{1,0:T(8,128)(2,1)} %q_in.1) | copy-start | bytes 589828
  2.9 0.7 copy-start.1

commit v2 on v1

v2 whole, which is shorter than its diff:
```python
import jax
import jax.numpy as jnp
from jax import lax
from jax.experimental import pallas as pl
from jax.experimental.pallas import tpu as pltpu
from jax.sharding import PartitionSpec as P

MESH = pl.DeviceIdType.MESH
SCALE = 20.0
DEAD = -1e30
GROUPS = 16
ROWS = 16
QUERIES = 128
WIDTH = 768
MATES = (8, 12, 4)
LEAVES = (-3, -2, -1, 1, 2, 3)
HALVES = (pl.ds(0, WIDTH // 2), pl.ds(WIDTH // 2, WIDTH // 2))
SHIFTS = tuple((dy, dx) for dy in range(4) for dx in range(4) if (dy, dx) != (0, 0))


def inside(h):
    return (h >= 0) & (h < GROUPS)


def feeds(hub, o, core):
    if o == -1:
        return hub >= 1
    if o == 1:
        return hub <= 14
    if o == -3:
        return hub == 3
    if o == 3:
        return hub == 12
    if o == -2:
        return ((core == 0) & (hub >= 2)) | (hub == 2) | (hub == 3)
    return ((core == 1) & (hub <= 13)) | (hub == 12) | (hub == 13)


def hub_offsets(z, core):
    second = jnp.where(core == 0, jnp.where(z >= 14, -2, 2), jnp.where(z <= 1, 2, -2))
    return jnp.where(z == 15, -3, 1), jnp.where(z == 0, 3, -1), second


def place(h):
    return (h % 4) * 4 + h // 4


def rows_of(index, count=1):
    return pl.ds(pl.multiple_of(index * ROWS, ROWS), count * ROWS)


def score(a, b):
    return SCALE * lax.dot_general(
        a, b, (((1,), (1,)), ((), ())), preferred_element_type=jnp.float32
    )


def over_rows(a, b):
    return lax.dot_general(a, b, (((0,), (0,)), ((), ())), preferred_element_type=jnp.float32)


def dot(a, b):
    return jnp.dot(a, b, preferred_element_type=jnp.float32)


def kernel(
    q_in, p_in, pos_in, lists_in, counts_in,
    dq_out, dp_out, loss_out,
    lists, counts, q_buf, pos_own, pos_sib, p_buf, o_buf, s_buf, so_buf, g_buf, go_buf,
    st_mine, st_sib, dq_mine, dq_send, dq_sib,
    d_buf, r_buf, do_buf, leaf_buf, hub_buf, sum_buf, relay_buf, far_buf, acc,
    loc_sem, line_recv, hub_send, wide_send, wide_recv, leaf_send, far_send, far_recv, plane_send, plane_recv,
    sib_send, sib_recv, d_send, d_recv, leaf_send2, leaf_recv2, hub_send2, hub_recv2,
    relay_send2, relay_recv2, far_send2, far_recv2,
):
    g = lax.axis_index("grp")
    d = lax.axis_index("dp")
    y, zh, x, c = d // 16, (d // 8) % 2, (d // 2) % 4, d % 2

    def at(yy, zz, xx, cc):
        return ((yy * 2 + zz) * 4 + xx) * 2 + cc

    def mate(m):
        a = g // 4
        if m == 4:
            b = a + 1 - 2 * (a % 2)
        elif m == 8:
            b = (a + 2) % 4
        else:
            b = 3 - a
        return b * 4 + g % 4

    sib = (g, at(y, zh, x, 1 - c))
    plane = [(g, at((y + dy) % 4, zh, (x + dx) % 4, c)) for dy, dx in SHIFTS]
    far = (mate(8), at(y, 1 - zh, x, c))
    my_slot = y * 4 + x
    home = place(g)
    family = (g % 4) * 4

    def copy(src, dst, send, recv, dev):
        return pltpu.make_async_remote_copy(
            src_ref=src, dst_ref=dst, send_sem=send, recv_sem=recv,
            device_id=dev, device_id_type=MESH,
        )

    def received(dst, sem):
        copy(dst, dst, sem, sem, sib).wait_recv()

    barrier = pltpu.get_barrier_semaphore()

    def tell(dev):
        pl.semaphore_signal(barrier, inc=1, device_id=dev, device_id_type=MESH)

    tell((mate(8), d))
    tell(far)
    tell((mate(4), d))
    expected = jnp.int32(4 + len(SHIFTS))
    for o in LEAVES:
        pair = inside(g + o) & (feeds(g, o, c) | feeds(g + o, -o, c))
        pl.when(pair)(lambda o=o: tell((g + o, d)))
        expected = expected + pair.astype(jnp.int32)
    for dev in plane:
        tell(dev)
    tell(sib)

    own = p_buf.at[rows_of(my_slot)]
    local = [
        pltpu.make_async_copy(p_in, own, loc_sem.at[0]),
        pltpu.make_async_copy(p_in, o_buf.at[rows_of(home)], loc_sem.at[1]),
        pltpu.make_async_copy(q_in, q_buf.at[pl.ds(0, QUERIES)], loc_sem.at[2]),
        pltpu.make_async_copy(pos_in, pos_own, loc_sem.at[3]),
        pltpu.make_async_copy(lists_in, lists, loc_sem.at[4]),
        pltpu.make_async_copy(counts_in, counts, loc_sem.at[5]),
    ]
    for cp in local:
        cp.start()
    for cp in local:
        cp.wait()
    pl.semaphore_wait(barrier, expected)

    mine = o_buf.at[rows_of(home)]

    hub_copy = copy(mine, mine, hub_send.at[0], line_recv.at[home], (mate(4), d))

    def wide_copy(h):
        block = o_buf.at[rows_of(home), HALVES[h]]
        return copy(block, block, wide_send.at[h], wide_recv.at[h], (mate(8), d))

    other = place(mate(8))
    pass_copy = copy(
        o_buf.at[rows_of(other)], o_buf.at[rows_of(other)], hub_send.at[1], line_recv.at[other],
        (mate(4), d),
    )

    def leaf_copy(i, j, slot):
        block = o_buf.at[rows_of(slot)]
        return copy(block, block, leaf_send.at[i, j], line_recv.at[slot], (g + LEAVES[j], d))

    def leaf_each(act):
        for j, o in enumerate(LEAVES):
            pl.when(feeds(g, o, c) & inside(g + o))(lambda j=j: act(j))

    far_slot = 16 + my_slot

    def far_copy(h):
        return copy(
            o_buf.at[rows_of(other), HALVES[h]], p_buf.at[rows_of(far_slot), HALVES[h]],
            far_send.at[h], far_recv.at[h], far,
        )

    def plane_copy(i):
        return copy(own, own, plane_send.at[2, i], plane_recv.at[2, i], plane[i])

    def plane_copy2(h, i):
        block = p_buf.at[rows_of(far_slot), HALVES[h]]
        return copy(block, block, plane_send.at[h, i], plane_recv.at[h, i], plane[i])

    wide_copy(0).start()
    wide_copy(1).start()
    hub_copy.start()
    for i in range(15):
        plane_copy(i).start()
    leaf_each(lambda j: leaf_copy(3, j, home).start())
    q_copy = copy(
        q_buf.at[pl.ds(0, QUERIES)], q_buf.at[pl.ds(QUERIES, QUERIES)],
        sib_send.at[0], sib_recv.at[0], sib,
    )
    pos_copy = copy(pos_own, pos_sib, sib_send.at[1], sib_recv.at[1], sib)
    q_copy.start()
    pos_copy.start()

    for i in (0, 2, 1):
        slot = place(mate(MATES[i]))
        if MATES[i] == 8:
            for h in range(2):
                wide_copy(h).wait_recv()
                far_copy(h).start()
            pass_copy.start()
        else:
            received(o_buf.at[rows_of(slot)], line_recv.at[slot])
        leaf_each(lambda j, i=i, slot=slot: leaf_copy(i, j, slot).start())

    q_copy.wait_recv()
    pos_copy.wait_recv()
    pos = jnp.concatenate([pos_own[...], pos_sib[...]], axis=1)

    def hits(part):
        i = lax.broadcasted_iota(jnp.int32, (256, 2 * QUERIES), 0)
        zz = zh + part - 2 * zh * part
        column = ((i >> 6) << 8) + zz * 128 + (((i >> 4) & 3) << 5) + c * 16 + (i & 15)
        return column == pos

    def part_score(part):
        s = score(p_buf[part * 256 : part * 256 + 256], q_buf[...])
        s_buf[part * 256 : part * 256 + 256] = s
        top = jnp.max(s, axis=0, keepdims=True)
        total = jnp.sum(jnp.exp(s - top), axis=0, keepdims=True)
        picked = jnp.sum(jnp.where(hits(part), s, 0.0), axis=0, keepdims=True)
        return top, total, picked

    def join(a, b):
        top = jnp.maximum(a[0], b[0])
        return top, a[1] * jnp.exp(a[0] - top) + b[1] * jnp.exp(b[0] - top)

    for i in range(15):
        plane_copy(i).wait_recv()
    top0, total0, picked0 = part_score(0)

    for h in range(2):
        far_copy(h).wait_recv()
        for i in range(15):
            plane_copy2(h, i).start()

    for o in (1, 2, 3):
        for r in range(4):
            slot = ((g + o) % 4) * 4 + r
            received(o_buf.at[rows_of(slot)], line_recv.at[slot])
    row = lax.broadcasted_iota(jnp.int32, (GROUPS * ROWS, QUERIES), 0)
    row_group = ((row >> 4) & 3) * 4 + (row >> 6)
    live = jnp.zeros((GROUPS * ROWS, QUERIES), jnp.bool_)
    for i in range(4):
        entry = jnp.where(i < counts[0, 0], lists[0, i], -1)
        live = live | (row_group == entry)
    outer = jnp.where(live, score(o_buf[...], q_buf[0:QUERIES]), DEAD)
    so_buf[...] = outer
    outer_max = jnp.max(outer, axis=0, keepdims=True)
    outer_sum = jnp.sum(jnp.exp(outer - outer_max), axis=0, keepdims=True)
    half = join((top0[:, :QUERIES], total0[:, :QUERIES]), (outer_max, outer_sum))
    top0 = jnp.concatenate([half[0], top0[:, QUERIES:]], axis=1)
    total0 = jnp.concatenate([half[1], total0[:, QUERIES:]], axis=1)

    for i in range(15):
        plane_copy2(0, i).wait_recv()
        plane_copy2(1, i).wait_recv()
    top1, total1, picked1 = part_score(1)
    top, total = join((top0, total0), (top1, total1))
    picked = picked0 + picked1
    st_mine[0:1] = top
    st_mine[1:2] = total
    st_mine[2:3] = picked
    st_mine[3:8] = jnp.zeros((5, 2 * QUERIES), jnp.float32)
    st_copy = copy(st_mine, st_sib, sib_send.at[2], sib_recv.at[2], sib)
    st_copy.start()

    hub_copy.wait_send()
    pass_copy.wait_send()
    for h in range(2):
        wide_copy(h).wait_send()
        far_copy(h).wait_send()
    for i in range(3):
        slot = place(mate(MATES[i]))
        leaf_each(lambda j, i=i, slot=slot: leaf_copy(i, j, slot).wait_send())
    leaf_each(lambda j: leaf_copy(3, j, home).wait_send())
    for i in range(15):
        plane_copy(i).wait_send()
        plane_copy2(0, i).wait_send()
        plane_copy2(1, i).wait_send()
    q_copy.wait_send()
    pos_copy.wait_send()

    st_copy.wait()
    swapped = jnp.concatenate([st_sib[:, QUERIES:], st_sib[:, :QUERIES]], axis=1)
    top, total = join((top, total), (swapped[0:1], swapped[1:2]))
    log_total = top + jnp.log(total)
    loss_out[...] = (log_total - (picked + swapped[2:3]))[:, :QUERIES]

    def part_grad(part):
        a = jnp.exp(s_buf[part * 256 : part * 256 + 256] - log_total)
        a = (a - hits(part).astype(jnp.float32)).astype(jnp.bfloat16)
        g_buf[part * 256 : part * 256 + 256] = a
        d_buf[part * 256 : part * 256 + 256] = (SCALE * dot(a, q_buf[...])).astype(jnp.bfloat16)

    def to_slot(i):
        dy, dx = SHIFTS[i]
        return ((y + dy) % 4) * 4 + (x + dx) % 4

    def d_copy(i):
        return copy(
            d_buf.at[rows_of(to_slot(i))], r_buf.at[0, i], d_send.at[2, i], d_recv.at[2, i],
            plane[i],
        )

    def d_copy2(h, i):
        return copy(
            d_buf.at[rows_of(16 + to_slot(i)), HALVES[h]], r_buf.at[1, i, pl.ds(0, ROWS), HALVES[h]],
            d_send.at[h, i], d_recv.at[h, i], plane[i],
        )

    hubs = hub_offsets(g, c)

    def leaf_back(j, h):
        to = g + hubs[j]
        return copy(
            do_buf.at[rows_of((to % 4) * 4, 4), HALVES[h]],
            leaf_buf.at[3 - hubs[j], pl.ds(0, 4 * ROWS), HALVES[h]],
            leaf_send2.at[j, h], leaf_recv2.at[3 - hubs[j], h], (to, d),
        )

    part_grad(1)
    for h in range(2):
        for i in range(15):
            d_copy2(h, i).start()
    a = jnp.where(live, jnp.exp(so_buf[...] - log_total[:, :QUERIES]), 0.0).astype(jnp.bfloat16)
    go_buf[...] = a
    do_buf[...] = (SCALE * dot(a, q_buf[0:QUERIES])).astype(jnp.bfloat16)
    for h in range(2):
        for j in range(3):
            leaf_back(j, h).start()
    part_grad(0)

    dq_send[...] = over_rows(g_buf[:, QUERIES:], p_buf[...])
    dq_copy = copy(dq_send, dq_sib, sib_send.at[3], sib_recv.at[3], sib)
    dq_copy.start()
    dq_mine[...] = over_rows(g_buf[:, :QUERIES], p_buf[...]) + over_rows(go_buf[...], o_buf[...])

    near_rows, wide_rows, far_rows = pl.ds(0, 32), pl.ds(32, 16), pl.ds(48, 16)

    def near_back(h):
        return copy(
            sum_buf.at[near_rows, HALVES[h]], hub_buf.at[near_rows, HALVES[h]],
            hub_send2.at[0, h], hub_recv2.at[0, h], (mate(4), d),
        )

    def wide_back(h):
        return copy(
            sum_buf.at[wide_rows, HALVES[h]], hub_buf.at[wide_rows, HALVES[h]],
            hub_send2.at[1, h], hub_recv2.at[1, h], (mate(8), d),
        )

    def relay_copy(h):
        return copy(
            sum_buf.at[far_rows, HALVES[h]], relay_buf.at[pl.ds(0, ROWS), HALVES[h]],
            relay_send2.at[h], relay_recv2.at[h], (mate(8), d),
        )

    def far_back(h):
        return copy(
            relay_buf.at[pl.ds(0, ROWS), HALVES[h]], far_buf.at[pl.ds(0, ROWS), HALVES[h]],
            far_send2.at[h], far_recv2.at[h], far,
        )

    def class_sum(m, cols):
        return acc[rows_of(place(mate(m)) - family), cols]

    for h, cols in enumerate(HALVES):
        acc[:, cols] = do_buf[rows_of(family, 4), cols].astype(jnp.float32)
        for o in LEAVES:

            @pl.when(feeds(g, o, c) & inside(g + o))
            def _(o=o, h=h, cols=cols):
                received(leaf_buf.at[o + 3, pl.ds(0, 4 * ROWS), cols], leaf_recv2.at[o + 3, h])
                acc[:, cols] += leaf_buf[o + 3, :, cols].astype(jnp.float32)

        sum_buf[0:16, cols] = class_sum(4, cols).astype(jnp.bfloat16)
        sum_buf[16:32, cols] = class_sum(12, cols).astype(jnp.bfloat16)
        near_back(h).start()
        total_far = d_buf[rows_of(far_slot), cols].astype(jnp.float32)
        for i in range(15):
            d_copy2(h, i).wait_recv()
            total_far = total_far + r_buf[1, i, :, cols].astype(jnp.float32)
        sum_buf[48:64, cols] = total_far.astype(jnp.bfloat16)
        relay_copy(h).start()

    for i in range(15):
        d_copy(i).start()

    for h, cols in enumerate(HALVES):
        near_back(h).wait_recv()
        sum_buf[32:48, cols] = (
            class_sum(8, cols) + hub_buf[16:32, cols].astype(jnp.float32)
        ).astype(jnp.bfloat16)
        wide_back(h).start()
        relay_copy(h).wait_recv()
        far_back(h).start()

    dq_copy.wait_recv()
    dq_out[...] = (SCALE * (dq_mine[...] + dq_sib[...])).astype(jnp.bfloat16)

    total_own = acc[rows_of(home - family)] + d_buf[rows_of(my_slot)].astype(jnp.float32)
    for i in range(15):
        d_copy(i).wait_recv()
        total_own = total_own + r_buf[0, i].astype(jnp.float32)
    for i in range(15):
        d_copy(i).wait_send()
        d_copy2(0, i).wait_send()
        d_copy2(1, i).wait_send()
    dq_copy.wait_send()
    for h in range(2):
        for j in range(3):
            leaf_back(j, h).wait_send()
        relay_copy(h).wait_send()
        near_back(h).wait_send()
        wide_back(h).wait_send()
    wide_back(0).wait_recv()
    wide_back(1).wait_recv()
    total_own = total_own + hub_buf[0:16].astype(jnp.float32) + hub_buf[32:48].astype(jnp.float32)
    for h in range(2):
        far_back(h).wait_send()
        far_back(h).wait_recv()
    dp_out[...] = (total_own + far_buf[...].astype(jnp.float32)).astype(jnp.bfloat16)


def per_device(query_emb, passage_emb, positives, hard_lists, hard_counts):
    bf16, f32, i32 = jnp.bfloat16, jnp.float32, jnp.int32
    dma = pltpu.SemaphoreType.DMA
    block = (ROWS, WIDTH)
    hbm = pl.BlockSpec(memory_space=pltpu.HBM)
    vmem = pl.BlockSpec(memory_space=pltpu.VMEM)
    dq, dp, loss = pl.pallas_call(
        kernel,
        out_shape=(
            jax.ShapeDtypeStruct((QUERIES, WIDTH), bf16),
            jax.ShapeDtypeStruct(block, bf16),
            jax.ShapeDtypeStruct((1, QUERIES), f32),
        ),
        in_specs=[hbm] * 5,
        out_specs=(vmem, vmem, vmem),
        scratch_shapes=[
            pltpu.SMEM((1, 4), i32),
            pltpu.SMEM((1, 1), i32),
            pltpu.VMEM((2 * QUERIES, WIDTH), bf16),
            pltpu.VMEM((1, QUERIES), i32),
            pltpu.VMEM((1, QUERIES), i32),
            pltpu.VMEM((512, WIDTH), bf16),
            pltpu.VMEM((256, WIDTH), bf16),
            pltpu.VMEM((512, 2 * QUERIES), f32),
            pltpu.VMEM((256, QUERIES), f32),
            pltpu.VMEM((512, 2 * QUERIES), bf16),
            pltpu.VMEM((256, QUERIES), bf16),
            pltpu.VMEM((8, 2 * QUERIES), f32),
            pltpu.VMEM((8, 2 * QUERIES), f32),
            pltpu.VMEM((QUERIES, WIDTH), f32),
            pltpu.VMEM((QUERIES, WIDTH), f32),
            pltpu.VMEM((QUERIES, WIDTH), f32),
            pltpu.VMEM((512, WIDTH), bf16),
            pltpu.VMEM((2, 15) + block, bf16),
            pltpu.VMEM((256, WIDTH), bf16),
            pltpu.VMEM((7, 4 * ROWS, WIDTH), bf16),
            pltpu.VMEM((3 * ROWS, WIDTH), bf16),
            pltpu.VMEM((4 * ROWS, WIDTH), bf16),
            pltpu.VMEM(block, bf16),
            pltpu.VMEM(block, bf16),
            pltpu.VMEM((4 * ROWS, WIDTH), f32),
            dma((6,)),
            dma((16,)),
            dma((2,)),
            dma((2,)),
            dma((2,)),
            dma((4, 6)),
            dma((2,)),
            dma((2,)),
            dma((3, 15)),
            dma((3, 15)),
            dma((4,)),
            dma((4,)),
            dma((3, 15)),
            dma((3, 15)),
            dma((3, 2)),
            dma((7, 2)),
            dma((2, 2)),
            dma((2, 2)),
            dma((2,)),
            dma((2,)),
            dma((2,)),
            dma((2,)),
        ],
        name="dual_encoder",
        compiler_params=pltpu.CompilerParams(
            collective_id=0, has_side_effects=True, vmem_limit_bytes=60 * 1024 * 1024
        ),
    )(
        query_emb, passage_emb, positives.reshape(1, QUERIES), hard_lists.reshape(1, 4),
        hard_counts,
    )
    return dq, dp, loss.reshape(QUERIES)


def solution(mesh):
    in_specs = (
        P(("grp", "dp"), None),
        P(("grp", "dp"), None),
        P(("grp", "dp")),
        P("grp", "dp", None),
        P("grp", "dp"),
    )
    out_specs = (P(("grp", "dp"), None), P(("grp", "dp"), None), P(("grp", "dp")))
    return jax.shard_map(
        per_device, mesh=mesh, in_specs=in_specs, out_specs=out_specs, check_vma=False
    )
```

time: 88.8 us -> 83.1 us (0.936)
  the two profiles are of different devices: /device:TPU:64 before, /device:TPU:1 now
where the time goes in v2:
time: 83.1 us; the launch traced here: 82.1 us
  Pallas kernels  78.1 us (94%)
  local copies, waits for them, and re-layouts  2.76 us (3%)
  between operations  1.3 us (2%)
    pallas_call x1, Pallas kernels, per_device(): pl.pallas_call(kernel, out_shape=(jax.ShapeDtypeStruct((QUERIES, WIDTH),...  78.1 us
    unnamed x7, local copies, waits for them, and re-layouts  2.76 us

profile of v2, /device:TPU:1, one launch (start us, length us, event | category | flops | bytes accessed | tf_op | source)
XLA Modules:
  0.0 82.1 jit_solution(16026780949197197044)
XLA Ops:
  1.3 78.1 %dual_encoder.1 = (bf16[128,768]{1,0:T(8,128)(2,1)}, bf16[16,768]{1,0:T(8,128)(2,1)}, f32[1,128]{1,0:T(1,128)}) custom-call(bf16[128,768]{1,0:T(8,128)(2,1)} %q_in.1, bf16[16,768]{1,0:T(8,128)(2,1)} %p_in.1, s32[1,128]{1,0:T(1,128)} %bitcast.3, s32[1,4]{1,0:T(1,128)} %bitcast.4, s32[1,1]{1,0:T(1,128)S(6)} %copy.11.counts_in), custom_call_target="tpu_custom_call" | custom-call | tf_op jit(solution)/shard_map/dual_encoder/pallas_call | solution.py:429
  79.3 0.0 copy-start
  79.4 1.6 %copy.12 = bf16[128,768]{1,0:T(8,128)(2,1)} copy(bf16[128,768]{1,0:T(8,128)(2,1)} %get-tuple-element.12) | data formatting | bytes 393216
  81.0 0.0 copy-done
  81.0 0.0 copy-start.1
  81.0 0.6 copy.13
  81.6 0.0 copy-done.1
  81.6 0.5 copy.14
Async XLA Ops:
  79.3 1.6 %copy-start = (bf16[16,768]{1,0:T(8,128)(2,1)S(1)}, bf16[16,768]{1,0:T(8,128)(2,1)}, u32[]{:S(2)}) copy-start(bf16[16,768]{1,0:T(8,128)(2,1)} %get-tuple-element.13) | copy-start | bytes 73732
  81.0 0.6 copy-start.1

commit v3 on v2

--- a/solution.py
+++ b/solution.py
@@ -316,16 +316,16 @@
             leaf_send2.at[j, h], leaf_recv2.at[3 - hubs[j], h], (to, d),
         )
 
-    part_grad(1)
-    for h in range(2):
-        for i in range(15):
-            d_copy2(h, i).start()
     a = jnp.where(live, jnp.exp(so_buf[...] - log_total[:, :QUERIES]), 0.0).astype(jnp.bfloat16)
     go_buf[...] = a
     do_buf[...] = (SCALE * dot(a, q_buf[0:QUERIES])).astype(jnp.bfloat16)
     for h in range(2):
         for j in range(3):
             leaf_back(j, h).start()
+    part_grad(1)
+    for h in range(2):
+        for i in range(15):
+            d_copy2(h, i).start()
     part_grad(0)
 
     dq_send[...] = over_rows(g_buf[:, QUERIES:], p_buf[...])

time: 83.1 us -> 84.3 us (1.014)
  Pallas kernels: 78.1 us -> 80 us
    pallas_call x1, Pallas kernels: 78.1 us -> 80 us  [per_device(): pl.pallas_call(kernel, out_shape=(jax.ShapeDtypeStruct((QUERIES, WIDTH),...]
where the time goes in v3:
time: 84.3 us; the launch traced here: 84.1 us
  Pallas kernels  80 us (95%)
  local copies, waits for them, and re-layouts  2.76 us (3%)
  between operations  1.3 us (2%)
    pallas_call x1, Pallas kernels, per_device(): pl.pallas_call(kernel, out_shape=(jax.ShapeDtypeStruct((QUERIES, WIDTH),...  80 us
    unnamed x7, local copies, waits for them, and re-layouts  2.76 us

profile of v3, /device:TPU:1, one launch (start us, length us, event | category | flops | bytes accessed | tf_op | source)
XLA Modules:
  0.0 84.1 jit_solution(11971637617987861515)
XLA Ops:
  1.3 80.0 %dual_encoder.1 = (bf16[128,768]{1,0:T(8,128)(2,1)}, bf16[16,768]{1,0:T(8,128)(2,1)}, f32[1,128]{1,0:T(1,128)}) custom-call(bf16[128,768]{1,0:T(8,128)(2,1)} %q_in.1, bf16[16,768]{1,0:T(8,128)(2,1)} %p_in.1, s32[1,128]{1,0:T(1,128)} %bitcast.3, s32[1,4]{1,0:T(1,128)} %bitcast.4, s32[1,1]{1,0:T(1,128)S(6)} %copy.11.counts_in), custom_call_target="tpu_custom_call" | custom-call | tf_op jit(solution)/shard_map/dual_encoder/pallas_call | solution.py:429
  81.3 0.0 copy-start
  81.3 1.6 %copy.12 = bf16[128,768]{1,0:T(8,128)(2,1)} copy(bf16[128,768]{1,0:T(8,128)(2,1)} %get-tuple-element.12) | data formatting | bytes 393216
  82.9 0.0 copy-done
  82.9 0.0 copy-start.1
  82.9 0.6 copy.13
  83.5 0.0 copy-done.1
  83.5 0.5 copy.14
Async XLA Ops:
  81.3 1.6 %copy-start = (bf16[16,768]{1,0:T(8,128)(2,1)S(1)}, bf16[16,768]{1,0:T(8,128)(2,1)}, u32[]{:S(2)}) copy-start(bf16[16,768]{1,0:T(8,128)(2,1)} %get-tuple-element.13) | copy-start | bytes 73732
  82.9 0.6 copy-start.1
